TPU v7x, 256 devices: a whole 4x4x8 slice. The times are simulated.
256 devices in a mesh: chan: 16 (over z, x_lo), freq: 16 (over x_hi, y, core).
Axes of the slice: x: 4 (x_hi: 2, x_lo: 2; x = x_hi * 2 + x_lo), y: 4, z: 8, core: 2. Of those that a mesh axis runs over, the one named last changes fastest.
Arguments:
- traces: bfloat16 [2048, 36864], P('chan', 'freq'), may hold values from -60 to 60
- starts: int32 [16], P('freq'), may hold values from 0 to 256
- mask: int32 [2048], P('chan'), may hold values 0 or 1
- pair_offsets: int32 [16, 3], P('chan'), may hold values from 0 to 8, as said below
Outputs:
- correlations: bfloat16 [16, 3, 128, 128, 1024], P('chan', None, 'freq')
Inputs may be any that keep to these rules, and one draw needn't show every extreme that they name: `pair_offsets`: each row holds 3 different offsets.
All inputs are finite; a program needn't handle non-finite values. No bound on the sum of `mask` on one device may be relied on, other than what follows from the above.
Results may differ from a plain program's by a relative error of at most 0.0066.
Values may be sent and summed in bfloat16 or wider, within the bound.
A program may use at most 128 MiB of HBM per device.

v0:
```python
import math

import jax
import jax.numpy as jnp
from jax import lax
from jax.sharding import PartitionSpec as P

BLK = 128
L = 2048
F = 512
KLO = 128
LAGS = 1024
K = 3
OFF = 8


def from_behind(shard, axis, by):
    count = lax.axis_size(axis)
    pairs = [(i, i + by) for i in range(count) if 0 <= i + by < count]
    return lax.ppermute(shard, axis, pairs)


def dft_table():
    samples = jnp.arange(L, dtype=jnp.int32)
    bin_ids = KLO + jnp.arange(F, dtype=jnp.int32)
    phase_idx = samples[:, None] * bin_ids[None, :] % L
    angles = 2.0 * math.pi / L * phase_idx.astype(jnp.float32)
    window_taper = 0.5 - 0.5 * jnp.cos(2.0 * math.pi / L * samples.astype(jnp.float32))
    real_cols = window_taper[:, None] * jnp.cos(angles)
    imag_cols = -window_taper[:, None] * jnp.sin(angles)
    return jnp.concatenate([real_cols, imag_cols], axis=1).astype(jnp.bfloat16)


def lag_table():
    bin_ids = KLO + jnp.arange(F, dtype=jnp.int32)
    delays = jnp.arange(LAGS, dtype=jnp.int32) - LAGS // 2
    phase_idx = bin_ids[:, None] * delays[None, :] % L
    angles = 2.0 * math.pi / L * phase_idx.astype(jnp.float32)
    return jnp.stack([jnp.cos(angles), -jnp.sin(angles)]).astype(jnp.bfloat16)


def cross_spectra(left_rows, right_rows):
    stacked = jnp.concatenate([left_rows[:, :, 0], left_rows[:, :, 1]], axis=1)
    rotated = jnp.concatenate([left_rows[:, :, 1], -left_rows[:, :, 0]], axis=1)
    partner = jnp.concatenate([right_rows[:, :, 0], right_rows[:, :, 1]], axis=1)
    real_part = jnp.einsum("iwf,jwf->fij", stacked, partner, preferred_element_type=jnp.float32)
    imag_part = jnp.einsum("iwf,jwf->fij", rotated, partner, preferred_element_type=jnp.float32)
    return jnp.stack([real_part, imag_part])


def on_device(traces, starts, mask, pair_offsets):
    channels = traces.shape[0]
    win_local = starts.shape[0]
    segment_len = traces.shape[1] // win_local
    windows = traces.reshape(channels, win_local, segment_len)
    segments = jax.vmap(
        lambda trace_rows, begin_at: lax.dynamic_slice_in_dim(trace_rows, begin_at, L, 1),
        in_axes=(1, 0),
        out_axes=1,
    )(windows, starts)
    spectra = jnp.dot(
        segments.reshape(channels * win_local, L), dft_table(), preferred_element_type=jnp.float32
    ).reshape(channels, win_local, 2, F)
    power_mean = jnp.sum(spectra * spectra, axis=(2, 3)) / F
    weight = lax.rsqrt(power_mean + 1e-06) * mask.astype(jnp.float32)[:, None]
    whitened = (spectra * weight[:, :, None, None]).astype(jnp.bfloat16)
    spread = lax.all_to_all(whitened, "freq", split_axis=3, concat_axis=1, tiled=True)
    blocks_local = pair_offsets.shape[0]
    all_windows = spread.shape[1]
    reach = (blocks_local + OFF - 1) // blocks_local
    collected = [spread]
    for shift_no in range(1, reach + 1):
        collected.append(from_behind(spread, "chan", -shift_no))
    extended = jnp.concatenate(collected, axis=0)
    flat_offsets = pair_offsets.reshape(-1)
    own_blocks = jnp.arange(blocks_local * K, dtype=jnp.int32) // K

    def pair_terms(own_no, offset):
        right_rows = lax.dynamic_slice_in_dim(extended, (own_no + offset) * BLK, BLK, 0)
        return cross_spectra(spread, right_rows)

    pair_spectra = jax.vmap(pair_terms)(own_blocks, flat_offsets).astype(jnp.bfloat16)
    pair_spectra = pair_spectra.reshape((blocks_local, K) + pair_spectra.shape[1:])
    lag_basis = lag_table()
    lag_scale = 1.0 / (all_windows * math.sqrt(F))
    lagged = jnp.einsum(
        "bkrfij,rfm->bkijm",
        lax.all_to_all(pair_spectra, "freq", split_axis=4, concat_axis=3, tiled=True),
        lag_basis,
        preferred_element_type=jnp.float32,
    )
    return (lagged * lag_scale).astype(jnp.bfloat16)


def solution(mesh):
    in_specs = (P("chan", "freq"), P("freq"), P("chan"), P("chan", None))
    out_specs = P("chan", None, "freq", None, None)
    return jax.shard_map(
        on_device, mesh=mesh, in_specs=in_specs, out_specs=out_specs, check_vma=False
    )
```

profile of v0, /device:TPU:61, one launch (start us, length us, event | category | flops | bytes accessed | tf_op | source)
XLA Modules:
  0.0 292.2 jit_solution(11999982150682971352)
XLA Ops:
  0.0 0.1 multiply_subtract_fusion
  0.8 17.7 %multiply_convert_fusion.1 = (bf16[2048,512]{1,0:T(8,128)(2,1)S(1)}, bf16[2048,512]{1,0:T(8,128)(2,1)S(1)}) fusion(s32[512]{0:T(512)S(1)} %iota_add_fusion.1, f32[2048]{0:T(1024)S(1)} %get-tuple-element.26, f32[2048]{0:T(1024)S(1)} %get-tuple-element.27), kind=kLoop, calls=%fused_computation.19 | loop fusion | flops 18874368 | bytes 4212736 | tf_op jit(solution)/shard_map/convert.6
  18.5 0.9 multiply_reduce_fusion
  19.3 0.2 copy.54
  19.5 0.2 copy.55
  19.8 0.1 multiply_convert_fusion.2
  19.9 0.9 copy.56
  20.7 7.4 %all-to-all-start = ((bf16[128,1,2,512]{0,2,1,3:T(2,128)(2,1)}), bf16[128,1,2,512]{0,2,1,3:T(2,128)(2,1)S(1)}, u32[]{:S(2)}, u32[]{:S(2)}) async-start(bf16[128,1,2,512]{0,2,1,3:T(2,128)(2,1)} %copy.56), calls=%async_computation | async-start | bytes 524288 | tf_op jit(solution)/shard_map/all_to_all | solution.py:67
  28.2 5.1 %all-to-all-done = bf16[128,1,2,512]{0,2,1,3:T(2,128)(2,1)S(1)} async-done(((bf16[128,1,2,512]{0,2,1,3:T(2,128)(2,1)}), bf16[128,1,2,512]{0,2,1,3:T(2,128)(2,1)S(1)}, u32[]{:S(2)}, u32[]{:S(2)}) %all-to-all-start) | async-done | bytes 262176 | tf_op jit(solution)/shard_map/all_to_all | solution.py:67
  33.3 0.2 copy.83
  33.5 0.2 constant_dynamic-update-slice_fusion.8
  33.7 2.4 collective-permute-start
  36.0 1.9 collective-permute-start.1
  38.0 1.3 collective-permute-start.2
  39.3 1.3 collective-permute-start.3
  40.6 1.3 collective-permute-start.4
  41.9 1.3 collective-permute-done
  43.3 1.3 collective-permute-start.5
  44.6 0.1 constant_dynamic-update-slice_fusion.7
  44.6 4.9 %collective-permute-done.1 = bf16[128,16,2,32]{0,1,3,2:T(8,128)(2,1)S(1)} collective-permute-done((bf16[128,16,2,32]{0,1,3,2:T(8,128)(2,1)S(1)}, bf16[128,16,2,32]{0,1,3,2:T(8,128)(2,1)S(1)}, u32[]{:S(2)}, u32[]{:S(2)}) %collective-permute-start.1) | collective-permute-done | bytes 262176 | tf_op jit(solution)/shard_map/ppermute | solution.py:20
  49.5 1.3 collective-permute-start.6
  50.8 0.1 constant_dynamic-update-slice_fusion.6
  50.9 1.2 collective-permute-done.2
  52.1 1.5 collective-permute-start.7
  53.5 0.1 constant_dynamic-update-slice_fusion.5
  53.6 10.5 %collective-permute-done.3 = bf16[128,16,2,32]{0,1,3,2:T(8,128)(2,1)S(1)} collective-permute-done((bf16[128,16,2,32]{0,1,3,2:T(8,128)(2,1)S(1)}, bf16[128,16,2,32]{0,1,3,2:T(8,128)(2,1)S(1)}, u32[]{:S(2)}, u32[]{:S(2)}) %collective-permute-start.3) | collective-permute-done | bytes 262176 | tf_op jit(solution)/shard_map/ppermute | solution.py:20
  64.1 0.1 constant_dynamic-update-slice_fusion.4
  64.2 2.4 collective-permute-done.4
  66.6 0.1 constant_dynamic-update-slice_fusion.3
  66.7 67.8 %collective-permute-done.5 = bf16[128,16,2,32]{0,1,3,2:T(8,128)(2,1)S(1)} collective-permute-done((bf16[128,16,2,32]{0,1,3,2:T(8,128)(2,1)S(1)}, bf16[128,16,2,32]{0,1,3,2:T(8,128)(2,1)S(1)}, u32[]{:S(2)}, u32[]{:S(2)}) %collective-permute-start.5) | collective-permute-done | bytes 262176 | tf_op jit(solution)/shard_map/ppermute | solution.py:20
  134.4 0.1 constant_dynamic-update-slice_fusion.2
  134.5 0.1 constant_dynamic-update-slice_fusion.1
  134.6 0.1 constant_dynamic-update-slice_fusion
  134.7 15.5 %copy.59 = bf16[1152,16,2,32]{3,1,2,0:T(8,128)(2,1)} copy(bf16[1152,16,2,32]{0,1,3,2:T(8,128)(2,1)S(1)} %constant_dynamic-update-slice_fusion) | data formatting | bytes 4718592 | tf_op jit(solution)/shard_map/concatenate | solution.py:74
  150.2 6.4 %gather_fusion = bf16[3,128,16,2,32]{4,2,3,1,0:T(8,128)(2,1)} fusion(bf16[1152,16,2,32]{3,1,2,0:T(8,128)(2,1)} %copy.59, s32[3]{0:T(128)S(1)} %fusion.31), kind=kCustom, calls=%fused_computation | custom fusion | bytes 1572912 | tf_op jit(solution)/shard_map/vmap()/gather | solution.py:79
  156.6 3.6 %fusion.38 = (bf16[3,128,16,1,32]{4,2,3,1,0:T(8,128)(2,1)}, bf16[3,128,16,1,32]{4,2,3,1,0:T(8,128)(2,1)S(1)}) fusion(bf16[3,128,16,2,32]{4,2,3,1,0:T(8,128)(2,1)} %gather_fusion), kind=kLoop, calls=%fused_computation.80 | loop fusion | bytes 1572864 | tf_op jit(solution)/shard_map/vmap()/slice | solution.py:45
  160.2 2.2 copy.72
  162.4 1.2 copy.73
  163.6 1.0 convert_bitcast_fusion.1
  164.6 1.0 convert_bitcast_fusion
  165.6 0.6 maximum_bitcast_fusion
  166.2 6.8 %copy.62 = bf16[1,3,2,32,128,128]{5,3,2,1,0,4:T(8,128)(2,1)} copy(bf16[1,3,2,32,128,128]{5,4,1,3,2,0:T(8,128)(2,1)S(1)} %maximum_bitcast_fusion) | data formatting | bytes 12582912 | tf_op jit(solution)/shard_map/reshape | solution.py:83
  173.0 7.6 %all-to-all-start.1 = ((bf16[1,3,2,32,128,128]{5,3,2,1,0,4:T(8,128)(2,1)}), bf16[1,3,2,32,128,128]{5,3,2,1,0,4:T(8,128)(2,1)}, u32[]{:S(2)}, u32[]{:S(2)}) async-start(bf16[1,3,2,32,128,128]{5,3,2,1,0,4:T(8,128)(2,1)} %copy.62), calls=%async_computation.1 | async-start | bytes 12582912 | tf_op jit(solution)/shard_map/all_to_all | solution.py:88
  180.6 9.0 %cosine_convert_fusion = (bf16[1,512,1024]{2,1,0:T(8,128)(2,1)S(1)}, bf16[1,512,1024]{2,1,0:T(8,128)(2,1)S(1)}) fusion(s32[1024]{0:T(1024)S(1)} %iota_add_fusion, s32[512]{0:T(512)S(1)} %iota_add_fusion.1), kind=kLoop, calls=%fused_computation.37 | loop fusion | flops 8912896 | bytes 2103296 | tf_op jit(solution)/shard_map/convert
  189.6 85.2 %all-to-all-done.1 = bf16[1,3,2,32,128,128]{5,3,2,1,0,4:T(8,128)(2,1)} async-done(((bf16[1,3,2,32,128,128]{5,3,2,1,0,4:T(8,128)(2,1)}), bf16[1,3,2,32,128,128]{5,3,2,1,0,4:T(8,128)(2,1)}, u32[]{:S(2)}, u32[]{:S(2)}) %all-to-all-start.1) | async-done | bytes 6291488 | tf_op jit(solution)/shard_map/all_to_all | solution.py:88
  274.8 6.8 %copy.82 = bf16[1,3,2,32,128,128]{5,4,3,2,1,0:T(8,128)(2,1)S(1)} copy(bf16[1,3,2,32,128,128]{5,3,2,1,0,4:T(8,128)(2,1)} %all-to-all-done.1) | data formatting | bytes 12582912 | tf_op jit(solution)/shard_map/all_to_all | solution.py:88
  281.7 1.7 copy.64
  283.4 8.7 %fusion.1 = bf16[1,3,8,128,1024]{4,3,2,1,0:T(8,128)(2,1)} fusion(bf16[3,2,512,8,128]{4,3,2,1,0:T(8,128)(2,1)S(1)} %bitcast.61, bf16[1,512,1024]{2,1,0:T(8,128)(2,1)S(1)} %get-tuple-element.21, bf16[1,512,1024]{2,1,0:T(8,128)(2,1)S(1)} %get-tuple-element.20), kind=kOutput, calls=%fused_computation.3 | convolution fusion | flops 6449790976 | bytes 14680064 | tf_op jit(solution)/shard_map/bkrfij,rfm->bkijm/dot_general | solution.py:86
  (16 shorter events, 0.1 us)
Async XLA Ops:
  0.0 18.4 %copy-start = (bf16[128,2304]{1,0:T(8,128)(2,1)S(1)}, bf16[128,2304]{1,0:T(8,128)(2,1)}, u32[]{:S(2)}) copy-start(bf16[128,2304]{1,0:T(8,128)(2,1)} %param.4) | copy-start | bytes 1769476
  18.5 1.3 copy-start.2
  19.3 8.8 %copy-start.3 = (s32[1,3]{1,0:T(1,128)S(1)}, s32[1,3]{1,0:T(1,128)}, u32[]{:S(2)}) copy-start(s32[1,3]{1,0:T(1,128)} %param.7) | copy-start | bytes 40
  20.7 12.6 %all-to-all-start = ((bf16[128,1,2,512]{0,2,1,3:T(2,128)(2,1)}), bf16[128,1,2,512]{0,2,1,3:T(2,128)(2,1)S(1)}, u32[]{:S(2)}, u32[]{:S(2)}) async-start(bf16[128,1,2,512]{0,2,1,3:T(2,128)(2,1)} %copy.56), calls=%async_computation | async-start | bytes 524288 | tf_op jit(solution)/shard_map/all_to_all | solution.py:67
  33.7 9.6 %collective-permute-start = (bf16[128,16,2,32]{0,1,3,2:T(8,128)(2,1)S(1)}, bf16[128,16,2,32]{0,1,3,2:T(8,128)(2,1)S(1)}, u32[]{:S(2)}, u32[]{:S(2)}) collective-permute-start(bf16[128,16,2,32]{0,1,3,2:T(8,128)(2,1)S(1)} %bitcast.69), channel_id=1, source_target_pairs={{16,0},{32,16},{48,32},{64,48},{80,64},{96,80},{112,96},{128,112},... | collective-permute-start | bytes 786440 | tf_op jit(solution)/shard_map/ppermute | solution.py:20
  36.0 13.5 %collective-permute-start.1 = (bf16[128,16,2,32]{0,1,3,2:T(8,128)(2,1)S(1)}, bf16[128,16,2,32]{0,1,3,2:T(8,128)(2,1)S(1)}, u32[]{:S(2)}, u32[]{:S(2)}) collective-permute-start(bf16[128,16,2,32]{0,1,3,2:T(8,128)(2,1)S(1)} %bitcast.70), channel_id=1, source_target_pairs={{32,0},{48,16},{64,32},{80,48},{96,64},{112,80},{128,96},{144,112}... | collective-permute-start | bytes 786440 | tf_op jit(solution)/shard_map/ppermute | solution.py:20
  38.0 14.1 %collective-permute-start.2 = (bf16[128,16,2,32]{0,1,3,2:T(8,128)(2,1)S(1)}, bf16[128,16,2,32]{0,1,3,2:T(8,128)(2,1)S(1)}, u32[]{:S(2)}, u32[]{:S(2)}) collective-permute-start(bf16[128,16,2,32]{0,1,3,2:T(8,128)(2,1)S(1)} %bitcast.71), channel_id=1, source_target_pairs={{48,0},{64,16},{80,32},{96,48},{112,64},{128,80},{144,96},{160,112... | collective-permute-start | bytes 786440 | tf_op jit(solution)/shard_map/ppermute | solution.py:20
  39.3 24.8 %collective-permute-start.3 = (bf16[128,16,2,32]{0,1,3,2:T(8,128)(2,1)S(1)}, bf16[128,16,2,32]{0,1,3,2:T(8,128)(2,1)S(1)}, u32[]{:S(2)}, u32[]{:S(2)}) collective-permute-start(bf16[128,16,2,32]{0,1,3,2:T(8,128)(2,1)S(1)} %bitcast.72), channel_id=1, source_target_pairs={{64,0},{80,16},{96,32},{112,48},{128,64},{144,80},{160,96},{176,11... | collective-permute-start | bytes 786440 | tf_op jit(solution)/shard_map/ppermute | solution.py:20
  40.6 26.0 %collective-permute-start.4 = (bf16[128,16,2,32]{0,1,3,2:T(8,128)(2,1)S(1)}, bf16[128,16,2,32]{0,1,3,2:T(8,128)(2,1)S(1)}, u32[]{:S(2)}, u32[]{:S(2)}) collective-permute-start(bf16[128,16,2,32]{0,1,3,2:T(8,128)(2,1)S(1)} %bitcast.73), channel_id=1, source_target_pairs={{80,0},{96,16},{112,32},{128,48},{144,64},{160,80},{176,96},{192,1... | collective-permute-start | bytes 786440 | tf_op jit(solution)/shard_map/ppermute | solution.py:20
  43.3 91.2 %collective-permute-start.5 = (bf16[128,16,2,32]{0,1,3,2:T(8,128)(2,1)S(1)}, bf16[128,16,2,32]{0,1,3,2:T(8,128)(2,1)S(1)}, u32[]{:S(2)}, u32[]{:S(2)}) collective-permute-start(bf16[128,16,2,32]{0,1,3,2:T(8,128)(2,1)S(1)} %bitcast.76), channel_id=1, source_target_pairs={{96,0},{112,16},{128,32},{144,48},{160,64},{176,80},{192,96},{208,... | collective-permute-start | bytes 786440 | tf_op jit(solution)/shard_map/ppermute | solution.py:20
  49.5 85.0 %collective-permute-start.6 = (bf16[128,16,2,32]{0,1,3,2:T(8,128)(2,1)S(1)}, bf16[128,16,2,32]{0,1,3,2:T(8,128)(2,1)S(1)}, u32[]{:S(2)}, u32[]{:S(2)}) collective-permute-start(bf16[128,16,2,32]{0,1,3,2:T(8,128)(2,1)S(1)} %bitcast.77), channel_id=1, source_target_pairs={{112,0},{128,16},{144,32},{160,48},{176,64},{192,80},{208,96},{224... | collective-permute-start | bytes 786440 | tf_op jit(solution)/shard_map/ppermute | solution.py:20
  52.1 82.5 %collective-permute-start.7 = (bf16[128,16,2,32]{0,1,3,2:T(8,128)(2,1)S(1)}, bf16[128,16,2,32]{0,1,3,2:T(8,128)(2,1)S(1)}, u32[]{:S(2)}, u32[]{:S(2)}) collective-permute-start(bf16[128,16,2,32]{0,1,3,2:T(8,128)(2,1)S(1)} %bitcast.78), channel_id=1, source_target_pairs={{128,0},{144,16},{160,32},{176,48},{192,64},{208,80},{224,96},{240... | collective-permute-start | bytes 786440 | tf_op jit(solution)/shard_map/ppermute | solution.py:20
  173.0 101.9 %all-to-all-start.1 = ((bf16[1,3,2,32,128,128]{5,3,2,1,0,4:T(8,128)(2,1)}), bf16[1,3,2,32,128,128]{5,3,2,1,0,4:T(8,128)(2,1)}, u32[]{:S(2)}, u32[]{:S(2)}) async-start(bf16[1,3,2,32,128,128]{5,3,2,1,0,4:T(8,128)(2,1)} %copy.62), calls=%async_computation.1 | async-start | bytes 12582912 | tf_op jit(solution)/shard_map/all_to_all | solution.py:88
  283.4 8.8 %copy-start.1 = (bf16[128,2304]{1,0:T(8,128)(2,1)S(1)}, bf16[128,2304]{1,0:T(8,128)(2,1)}, u32[]{:S(2)}) copy-start(bf16[128,2304]{1,0:T(8,128)(2,1)} %param.4) | copy-start | bytes 1769476
where the time goes:
time: 293 us; the launch traced here: 292 us
  waiting for transfers between devices  178 us (61%)
  local copies, waits for them, and re-layouts  46.4 us (16%)
  other arithmetic  27.5 us (9%)
  starting transfers between devices  27.2 us (9%)
  matrix products  11.7 us (4%)
    ppermute x8, waiting for transfers between devices, from_behind(): return lax.ppermute(shard, axis, pairs)  88.1 us
    all_to_all x1, waiting for transfers between devices, on_device(): lax.all_to_all(pair_spectra, 'freq', split_axis=4, concat_axis=3, tiled=T...  85.2 us
    another operation x2, other arithmetic  26.7 us
    concatenate x2, local copies, waits for them, and re-layouts, on_device(): extended = jnp.concatenate(collected, axis=0)  15.6 us
    ppermute x8, starting transfers between devices, from_behind(): return lax.ppermute(shard, axis, pairs)  12.2 us
    dot_general x1, matrix products, on_device(): jnp.einsum('bkrfij,rfm->bkijm', lax.all_to_all(pair_spectra, 'freq', spli...  8.74 us
    all_to_all x2, local copies, waits for them, and re-layouts, on_device(): lax.all_to_all(pair_spectra, 'freq', split_axis=4, concat_axis=3, tiled=T...  8.57 us
    all_to_all x1, starting transfers between devices, on_device(): lax.all_to_all(pair_spectra, 'freq', split_axis=4, concat_axis=3, tiled=T...  7.59 us
  transfers between devices with their start and end apart: 10, of which 8 were waited for; matrix products, arithmetic and copies ran while one was open for 3% of the time, Pallas kernels for 0%

commit v1 on v0

v1 whole, which is shorter than its diff:
```python
import functools
import math

import jax
import jax.numpy as jnp
import ml_dtypes
import numpy as np
from jax import lax
from jax.experimental import pallas as pl
from jax.experimental.pallas import tpu as pltpu
from jax.sharding import PartitionSpec as P

BLK = 128
NB = 16
W = 16
L = 2048
SEG = 2304
F = 512
KLO = 128
LAGS = 1024
K = 3
ROWS = 2 * F
NQ = 4
RQ = ROWS // NQ
GQ = RQ // 16
MESH = pl.DeviceIdType.MESH
BF16 = jnp.bfloat16
F32 = jnp.float32


def dft_table():
    samples = np.arange(L, dtype=np.int64)
    bin_ids = KLO + np.arange(F, dtype=np.int64)
    angles = 2.0 * np.pi / L * (samples[:, None] * bin_ids[None, :] % L)
    taper = 0.5 - 0.5 * np.cos(2.0 * np.pi / L * samples)
    both = np.stack([taper[:, None] * np.cos(angles), -taper[:, None] * np.sin(angles)], axis=2)
    return both.reshape(L, ROWS).astype(np.float32).astype(ml_dtypes.bfloat16)


def lag_table():
    bin_ids = KLO + np.arange(F, dtype=np.int64)
    delays = np.arange(LAGS, dtype=np.int64) - LAGS // 2
    angles = 2.0 * np.pi / L * (bin_ids[:, None] * delays[None, :] % L)
    both = np.stack([np.cos(angles), -np.sin(angles)], axis=1)
    return both.reshape(ROWS, LAGS).astype(np.float32).astype(ml_dtypes.bfloat16)


def spectra_kernel(start_ref, traces_ref, mask_ref, basis_ref, by_bin_ref, by_owner_ref):
    shifted = pltpu.roll(traces_ref[...].astype(F32), lax.rem(SEG - start_ref[0], SEG), 1)
    segment = shifted[:, :L].astype(BF16)
    spectra = jnp.dot(segment, basis_ref[...], preferred_element_type=F32)
    power_mean = jnp.sum(spectra * spectra, axis=1, keepdims=True) / F
    weight = lax.rsqrt(power_mean + 1e-06) * mask_ref[...].astype(F32)
    whitened = spectra * weight
    by_bin_ref[...] = whitened.T.astype(BF16)
    for owner in range(16):
        rows = whitened[8 * owner : 8 * owner + 8]
        by_owner_ref[owner] = jnp.concatenate([rows[:, :F], rows[:, F:]], axis=0).astype(BF16)


def pairs_kernel(
    offsets_ref, own_ref, by_owner_ref, out_ref,
    near0, near1, near2, near3, held, rows_in, left, terms, turned,
    chain_send, chain_recv, side_send, side_recv, own_send, own_recv, pass_send, pass_recv, out_sem,
):
    near = [near0, near1, near2, near3]
    chan = lax.axis_index("chan")
    freq = lax.axis_index("freq")
    x_lo = lax.rem(chan, 2)
    core = lax.rem(freq, 2)
    y = lax.rem(freq // 2, 4)
    x_hi = freq // 8

    def window(hi, at_y, at_core):
        return hi * 8 + lax.rem(at_y, 4) * 2 + at_core

    below = (lax.rem(chan + 14, 16), freq)
    above = (lax.rem(chan + 2, 16), freq)
    beside = (chan + 1 - 2 * x_lo, freq)
    sibling = (chan, window(x_hi, y, 1 - core))
    across = (chan, window(1 - x_hi, y, core))
    y_up = (chan, window(x_hi, y + 1, core))
    y_down = (chan, window(x_hi, y + 3, core))
    peers = [(chan, lax.rem(freq + shift, 16)) for shift in range(1, 16)]

    barrier = pltpu.get_barrier_semaphore()
    everyone = peers + [below, above, beside]
    for other in everyone:
        pl.semaphore_signal(barrier, inc=1, device_id=other, device_id_type=MESH)
    for q in range(NQ):
        near[q][0] = own_ref[RQ * q : RQ * (q + 1), :]
    rows_in[freq] = by_owner_ref[freq]
    pl.semaphore_wait(barrier, len(everyone))

    def remote(src, dst, send, recv, device):
        return pltpu.make_async_remote_copy(
            src_ref=src, dst_ref=dst, send_sem=send, recv_sem=recv, device_id=device, device_id_type=MESH
        )

    def chain(hop, q):
        return remote(near[q].at[hop - 1], near[q].at[hop], chain_send.at[q, hop - 1], chain_recv.at[q, hop - 1], below)

    def side(hop, q):
        return remote(near[q].at[hop - x_lo], near[q].at[4 + hop], side_send.at[q, hop - 1], side_recv.at[q, hop - 1], beside)

    def owner_rows(shift):
        there = lax.rem(freq + shift, 16)
        return remote(by_owner_ref.at[there], rows_in.at[freq], own_send.at[shift - 1], own_recv.at[shift - 1], (chan, there))

    def wave(step):
        for q in range(NQ):
            hop = step - 2 * q
            if hop == 0:
                chain(1, q).start()
            if 1 <= hop <= 4:
                chain(hop, q).wait_recv()
                if hop < 4:
                    chain(hop + 1, q).start()
                side(hop, q).start()

    mine = window(x_hi, y, core)
    other_hi = window(1 - x_hi, y, core)

    own_before = window(x_hi, y + 3, core)
    own_after = window(x_hi, y + 1, core)
    other_before = window(1 - x_hi, y + 3, core)
    other_after = window(1 - x_hi, y + 1, core)
    own_far = window(x_hi, y + 2, core)
    other_far = window(1 - x_hi, y + 2, core)
    table = [
        (mine, across), (mine, y_up), (mine, y_down), (other_hi, y_up), (other_hi, y_down),
        (own_before, y_up), (other_after, y_down),
        (mine, sibling), (other_hi, sibling), (own_before, sibling), (own_after, sibling),
        (other_before, sibling), (other_after, sibling), (own_far, sibling), (other_far, sibling),
    ]

    def spread(q, no):
        which, device = table[no]
        return remote(held.at[q, which], held.at[q, which], pass_send.at[q, no], pass_recv.at[q, no], device)

    def phase_a(q):
        for hop in range(1, 5):
            side(hop, q).wait_recv()
        for slot in range(K):
            offset = offsets_ref[slot]
            odd = lax.rem(offset, 2)
            place = offset // 2 + odd * 5
            rows = near[q][place]
            held[q, mine, slot] = jnp.where(chan + offset < NB, rows, jnp.zeros_like(rows))
        for no in (0, 1, 2, 7):
            spread(q, no).start()

    def phase_b(q):
        spread(q, 0).wait_recv()
        for no in (3, 4, 8):
            spread(q, no).start()

    def phase_c(q):
        spread(q, 1).wait_recv()
        spread(q, 5).start()
        spread(q, 9).start()
        spread(q, 2).wait_recv()
        spread(q, 10).start()
        spread(q, 4).wait_recv()
        spread(q, 6).start()
        spread(q, 12).start()
        spread(q, 3).wait_recv()
        spread(q, 11).start()

    def phase_d(q):
        spread(q, 5).wait_recv()
        spread(q, 13).start()
        spread(q, 6).wait_recv()
        spread(q, 14).start()

    def out_copy(q):
        return pltpu.make_async_copy(turned.at[q % 2], out_ref.at[:, :, pl.ds(RQ * q, RQ)], out_sem.at[q % 2])

    def phase_e(q):
        for no in range(7, 15):
            spread(q, no).wait_recv()

        def group(g, carry):
            at = pl.ds(pl.multiple_of(g * 16, 16), 16)
            right = jnp.concatenate([held[q, :, slot, at, :].reshape(256, BLK) for slot in range(K)], axis=1)
            both = jnp.dot(left[q * GQ + g], right, preferred_element_type=F32)
            for slot in range(K):
                terms[slot, :, at, :] = both[:, BLK * slot : BLK * (slot + 1)].astype(BF16).reshape(8, 16, BLK)
            return carry

        lax.fori_loop(0, GQ, group, 0)
        if q >= 2:
            out_copy(q - 2).wait()

        def turn(n, carry):
            turned[q % 2, n] = terms[n // 8, lax.rem(n, 8)].T
            return carry

        lax.fori_loop(0, K * 8, turn, 0)
        out_copy(q).start()

    def build_left():
        for shift in range(1, 16):
            owner_rows(shift).wait_recv()
        lane = lax.broadcasted_iota(jnp.int32, (16, 128), 1)
        row = lax.broadcasted_iota(jnp.int32, (16, 128), 0)
        same_bin = (lane % 16) // 2 == row // 2
        even_row = row % 2 == 0
        slab = lane // 16
        even_lane = lane % 2 == 0

        def step(n, carry):
            v = n // 8
            s = lax.rem(n, 8)
            for half in range(2):
                got = jnp.zeros((16, 128), F32)
                for w in range(8):
                    part = rows_in[half * 8 + w, :, pl.ds(pl.multiple_of(v * 128, 128), 128)].astype(F32)
                    got = jnp.where(slab == w, pltpu.roll(part, lax.rem(16 * (w + 8 - s), 128), 1), got)
                swapped = jnp.where(even_lane, pltpu.roll(got, 127, 1), -pltpu.roll(got, 1, 1))
                for h in range(2):
                    for i in range(8):
                        r = slice(h * 8 + i, h * 8 + i + 1)
                        value = jnp.where(even_row, got[r], swapped[r])
                        left[h * 32 + n, 16 * i : 16 * i + 16, 128 * half : 128 * half + 128] = jnp.where(
                            same_bin, value, 0.0
                        ).astype(BF16)
            return carry

        lax.fori_loop(0, 32, step, 0)

    wave(0)
    for shift in range(1, 16):
        owner_rows(shift).start()
    wave(1)
    wave(2)
    wave(3)
    wave(4)
    phase_a(0)
    phase_b(0)
    wave(5)
    build_left()
    wave(6)
    phase_a(1)
    phase_c(0)
    phase_b(1)
    wave(7)
    phase_d(0)
    wave(8)
    phase_a(2)
    phase_c(1)
    phase_e(0)
    phase_b(2)
    wave(9)
    phase_d(1)
    wave(10)
    phase_a(3)
    phase_c(2)
    phase_e(1)
    phase_b(3)
    phase_d(2)
    phase_c(3)
    phase_e(2)
    phase_d(3)
    phase_e(3)

    for q in range(NQ):
        for hop in range(1, 5):
            chain(hop, q).wait_send()
            side(hop, q).wait_send()
        for no in range(len(table)):
            spread(q, no).wait_send()
    for shift in range(1, 16):
        owner_rows(shift).wait_send()
    out_copy(2).wait()
    out_copy(3).wait()


def on_device(traces, starts, mask, pair_offsets):
    vmem = pl.BlockSpec(memory_space=pltpu.VMEM)
    smem = pl.BlockSpec(memory_space=pltpu.SMEM)
    by_bin, by_owner = pl.pallas_call(
        spectra_kernel,
        name="spectra",
        out_shape=(jax.ShapeDtypeStruct((ROWS, BLK), BF16), jax.ShapeDtypeStruct((16, 16, F), BF16)),
        in_specs=[smem, vmem, vmem, vmem],
        out_specs=(vmem, vmem),
        compiler_params=pltpu.CompilerParams(vmem_limit_bytes=32 * 2**20),
    )(starts, traces, mask.reshape(BLK, 1), jnp.asarray(dft_table()))
    dma = pltpu.SemaphoreType.DMA
    pair_spectra = pl.pallas_call(
        pairs_kernel,
        name="pairs",
        out_shape=jax.ShapeDtypeStruct((K * 8, BLK, ROWS), BF16),
        in_specs=[smem, vmem, vmem],
        out_specs=pl.BlockSpec(memory_space=pl.ANY),
        scratch_shapes=[pltpu.VMEM((9, RQ, BLK), BF16)] * NQ
        + [
            pltpu.VMEM((NQ, 16, K, RQ, BLK), BF16),
            pltpu.VMEM((16, 16, F), BF16),
            pltpu.VMEM((ROWS // 16, 128, 256), BF16),
            pltpu.VMEM((K, 8, RQ, BLK), BF16),
            pltpu.VMEM((2, K * 8, BLK, RQ), BF16),
            dma((NQ, 4)), dma((NQ, 4)), dma((NQ, 4)), dma((NQ, 4)),
            dma((15,)), dma((15,)), dma((NQ, 15)), dma((NQ, 15)), dma((2,)),
        ],
        compiler_params=pltpu.CompilerParams(
            collective_id=0, has_side_effects=True, vmem_limit_bytes=48 * 2**20
        ),
    )(pair_offsets.reshape(K), by_bin, by_owner)
    lagged = jnp.dot(
        pair_spectra.reshape(K * 8 * BLK, ROWS), jnp.asarray(lag_table()), preferred_element_type=F32
    )
    lag_scale = 1.0 / (W * math.sqrt(F))
    return (lagged * lag_scale).astype(BF16).reshape(1, K, 8, BLK, LAGS)


def solution(mesh):
    in_specs = (P("chan", "freq"), P("freq"), P("chan"), P("chan", None))
    out_specs = P("chan", None, "freq", None, None)
    return jax.shard_map(
        on_device, mesh=mesh, in_specs=in_specs, out_specs=out_specs, check_vma=False
    )
```

time: 293 us -> 119 us (0.41)
  the two profiles are of different devices: /device:TPU:61 before, /device:TPU:1 now
where the time goes in v1:
time: 119 us
  Pallas kernels  102 us (86%)
  matrix products  11.4 us (10%)
  local copies, waits for them, and re-layouts  4.66 us (4%)
    pallas_call x1, Pallas kernels, on_device(): pl.pallas_call(pairs_kernel, name='pairs', out_shape=jax.ShapeDtypeStruct...  101 us
    dot_general x1, matrix products, on_device(): jnp.dot(pair_spectra.reshape(K * 8 * BLK, ROWS), jnp.asarray(lag_table())...  11.4 us
    unnamed x8, local copies, waits for them, and re-layouts  3.9 us

profile of v1, /device:TPU:1, one launch (start us, length us, event | category | flops | bytes accessed | tf_op | source)
XLA Modules:
  0.0 118.8 jit_solution(11037550798766552730)
XLA Ops:
  0.7 0.8 copy.7.mask_ref
  1.4 0.0 copy-start
  1.4 2.2 %copy-done = bf16[2048,1024]{1,0:T(8,128)(2,1)S(1)} copy-done((bf16[2048,1024]{1,0:T(8,128)(2,1)S(1)}, bf16[2048,1024]{1,0:T(8,128)(2,1)}, u32[]{:S(2)}) %copy-start) | copy-done | bytes 4194328
  3.6 0.0 copy-start.1
  3.6 1.1 copy-done.1
  4.7 0.0 copy-start.3
  4.7 1.2 %spectra.1 = (bf16[1024,128]{1,0:T(8,128)(2,1)S(1)}, bf16[16,16,512]{2,1,0:T(8,128)(2,1)S(1)}) custom-call(s32[1]{0:T(128)S(6)} %copy.8.start_ref, bf16[128,2304]{1,0:T(8,128)(2,1)S(1)} %copy-done.1, s32[128,1]{1,0:T(8,128)S(1)} %copy.7.mask_ref, bf16[2048,1024]{1,0:T(8,128)(2,1)S(1)} %copy-done), custom_call_target="tpu_custom_call" | custom-call | tf_op jit(solution)/shard_map/spectra/pallas_call | solution.py:282
  5.9 0.0 copy-start.2
  5.9 0.6 copy-done.2
  6.6 100.8 %pairs.1 = bf16[24,128,1024]{2,1,0:T(8,128)(2,1)} custom-call(s32[3]{0:T(128)S(1)} %bitcast.6, bf16[1024,128]{1,0:T(8,128)(2,1)S(1)} %get-tuple-element.7.own_ref, bf16[16,16,512]{2,1,0:T(8,128)(2,1)S(1)} %get-tuple-element.8.by_owner_ref), custom_call_target="tpu_custom_call" | custom-call | tf_op jit(solution)/shard_map/pairs/pallas_call | solution.py:291
  107.4 0.0 copy-done.3
  107.4 11.4 %multiply_convert_fusion = bf16[3072,1024]{1,0:T(8,128)(2,1)} fusion(bf16[3072,1024]{1,0:T(8,128)(2,1)} %bitcast.7, bf16[1024,1024]{1,0:T(8,128)(2,1)S(1)} %copy-done.3), kind=kOutput, calls=%fused_computation | convolution fusion | flops 6448742400 | bytes 14680064 | tf_op jit(solution)/shard_map/dot_general | solution.py:311
Async XLA Ops:
  1.4 2.2 %copy-start = (bf16[2048,1024]{1,0:T(8,128)(2,1)S(1)}, bf16[2048,1024]{1,0:T(8,128)(2,1)}, u32[]{:S(2)}) copy-start(bf16[2048,1024]{1,0:T(8,128)(2,1)} %constant.6.clone.basis_ref) | copy-start | bytes 12582916
  3.6 1.1 copy-start.1
  4.7 102.7 %copy-start.3 = (bf16[1024,1024]{1,0:T(8,128)(2,1)S(1)}, bf16[1024,1024]{1,0:T(8,128)(2,1)}, u32[]{:S(2)}) copy-start(bf16[1024,1024]{1,0:T(8,128)(2,1)} %constant.7.clone) | copy-start | bytes 6291460
  5.9 0.7 copy-start.2

commit v2 on v1

v2 whole, which is shorter than its diff:
```python
import functools
import math

import jax
import jax.numpy as jnp
import ml_dtypes
import numpy as np
from jax import lax
from jax.experimental import pallas as pl
from jax.experimental.pallas import tpu as pltpu
from jax.sharding import PartitionSpec as P

BLK = 128
NB = 16
W = 16
L = 2048
SEG = 2304
F = 512
KLO = 128
LAGS = 1024
K = 3
ROWS = 2 * F
SIZES = (128, 128, 192, 192, 192, 192)
NQ = len(SIZES)
FIRST = tuple(sum(SIZES[:q]) for q in range(NQ))
TURNED = (0, 1, 2, 3)
VMEM_MIB = 60
MESH = pl.DeviceIdType.MESH
BF16 = jnp.bfloat16
F32 = jnp.float32


def dft_table():
    samples = np.arange(L, dtype=np.int64)
    bin_ids = KLO + np.arange(F, dtype=np.int64)
    angles = 2.0 * np.pi / L * (samples[:, None] * bin_ids[None, :] % L)
    taper = 0.5 - 0.5 * np.cos(2.0 * np.pi / L * samples)
    both = np.stack([taper[:, None] * np.cos(angles), -taper[:, None] * np.sin(angles)], axis=2)
    return both.reshape(L, ROWS).astype(np.float32).astype(ml_dtypes.bfloat16)


def lag_table():
    bin_ids = KLO + np.arange(F, dtype=np.int64)
    delays = np.arange(LAGS, dtype=np.int64) - LAGS // 2
    angles = 2.0 * np.pi / L * (bin_ids[:, None] * delays[None, :] % L)
    both = np.stack([np.cos(angles), -np.sin(angles)], axis=1)
    return both.reshape(ROWS, LAGS).astype(np.float32).astype(ml_dtypes.bfloat16)


class Tracked:
    def __init__(self, key, copy, started, waited):
        self.key, self.copy, self.started, self.waited = key, copy, started, waited

    def start(self):
        self.copy.start()
        self.started[self.key] = self.copy

    def wait_recv(self):
        self.copy.wait_recv()
        self.waited.add(self.key)


SCHEDULE = (
    "s0", "o", "w10", "s1", "w20", "l0", "w11", "s2", "l1", "w30", "l2", "w21", "l3", "w12", "s3", "w40", "w31",
    "w22", "w13", "s4", "a0", "w41", "w32", "w23", "w14", "s5", "a1", "b0", "c0", "C0", "w42", "w33", "w24",
    "w15", "b1", "c1", "C1", "w43", "a2", "w34", "k0", "K0", "w25", "d0", "a3", "w44", "k1", "K1", "w35", "d1",
    "b2", "w45", "h0", "c2", "C2", "a4", "e0", "f00", "b3", "c3", "C3", "f01", "h1", "a5", "k2", "K2", "e1",
    "f10", "b4", "d2", "f11", "c4", "C4", "b5", "k3", "K3", "h2", "d3", "e2", "f20", "c5", "C5", "f21", "h3",
    "k4", "K4", "e3", "f30", "d4", "k5", "f31", "h4", "K5", "e4", "f40", "d5", "h5", "f41", "e5", "f50", "f51",
)


def correlate_kernel(
    schedule, starts_hbm, traces_hbm, mask_hbm, offsets_hbm, basis_hbm, lag_hbm, out_ref,
    *scratch,
):
    near = scratch[:NQ]
    held = scratch[NQ : 2 * NQ]
    theirs = scratch[2 * NQ : 3 * NQ]
    (
        by_owner, rows_in, left, terms, total, done, out_sem,
        starts_ref, traces_ref, mask_ref, offsets_ref, beside_offsets, lag_ref, load_sem, asked_send, asked_recv,
        chain_send, chain_recv, side_send, side_recv, own_send, own_recv, pass_send, pass_recv,
    ) = scratch[3 * NQ :]
    basis_ref = left
    operands = [
        (starts_hbm, starts_ref), (traces_hbm, traces_ref), (mask_hbm, mask_ref),
        (basis_hbm, basis_ref), (offsets_hbm, offsets_ref), (lag_hbm, lag_ref),
    ]
    loads = [pltpu.make_async_copy(src, dst, load_sem.at[no]) for no, (src, dst) in enumerate(operands)]
    for load in loads:
        load.start()
    chan = lax.axis_index("chan")
    freq = lax.axis_index("freq")
    x_lo = lax.rem(chan, 2)
    core = lax.rem(freq, 2)
    y = lax.rem(freq // 2, 4)
    x_hi = freq // 8

    def window(hi, at_y, at_core):
        return hi * 8 + lax.rem(at_y, 4) * 2 + at_core

    below = (lax.rem(chan + 14, 16), freq)
    above = (lax.rem(chan + 2, 16), freq)
    beside = (chan + 1 - 2 * x_lo, freq)
    sibling = (chan, window(x_hi, y, 1 - core))
    across = (chan, window(1 - x_hi, y, core))
    diagonal = (chan + 1 - 2 * x_lo, window(1 - x_hi, y, core))
    y_up = (chan, window(x_hi, y + 1, core))
    y_down = (chan, window(x_hi, y + 3, core))
    peers = [(chan, lax.rem(freq + shift, 16)) for shift in range(1, 16)]

    started, waited = {}, set()
    barrier = pltpu.get_barrier_semaphore()
    everyone = peers + [below, above, beside, diagonal]
    for other in everyone:
        pl.semaphore_signal(barrier, inc=1, device_id=other, device_id_type=MESH)
    for load in loads[:4]:
        load.wait()
    shifted = pltpu.roll(traces_ref[...].astype(F32), lax.rem(SEG - starts_ref[0], SEG), 1)
    spectra = jnp.dot(shifted[:, :L].astype(BF16), basis_ref[...], preferred_element_type=F32)
    power_mean = jnp.sum(spectra * spectra, axis=1, keepdims=True) / F
    working = jnp.broadcast_to(mask_ref[...].astype(F32), (BLK, BLK)).T[:, :1]
    whitened = spectra * (lax.rsqrt(power_mean + 1e-06) * working)
    by_bin = whitened.T.astype(BF16)
    for q in range(NQ):
        near[q][0] = by_bin[FIRST[q] : FIRST[q] + SIZES[q], :]
    for owner in range(16):
        rows = whitened[8 * owner : 8 * owner + 8]
        by_owner[owner] = jnp.concatenate([rows[:, :F], rows[:, F:]], axis=0).astype(BF16)
    rows_in[freq] = by_owner[freq]
    loads[4].wait()
    loads[5].wait()
    pl.semaphore_wait(barrier, len(everyone))

    def remote(key, src, dst, send, recv, device):
        copy = pltpu.make_async_remote_copy(
            src_ref=src, dst_ref=dst, send_sem=send, recv_sem=recv, device_id=device, device_id_type=MESH
        )
        return Tracked(key, copy, started, waited)

    def chain(hop, q):
        return remote(("chain", hop, q), near[q].at[hop - 1], near[q].at[hop], chain_send.at[q, hop - 1], chain_recv.at[q, hop - 1], below)

    def side(hop, q):
        return remote(("side", hop, q), near[q].at[hop], near[q].at[5 + hop], side_send.at[q, hop], side_recv.at[q, hop], beside)

    def owner_rows(shift):
        there = lax.rem(freq + shift, 16)
        return remote(("own", shift), by_owner.at[there], rows_in.at[freq], own_send.at[shift - 1], own_recv.at[shift - 1], (chan, there))

    def begin(q):
        chain(1, q).start()
        side(0, q).start()

    def pass_on(hop, q):
        chain(hop, q).wait_recv()
        if hop < 4:
            chain(hop + 1, q).start()
        side(hop, q).start()

    mine = window(x_hi, y, core)
    other_hi = window(1 - x_hi, y, core)

    own_before = window(x_hi, y + 3, core)
    own_after = window(x_hi, y + 1, core)
    other_before = window(1 - x_hi, y + 3, core)
    other_after = window(1 - x_hi, y + 1, core)
    own_far = window(x_hi, y + 2, core)
    other_far = window(1 - x_hi, y + 2, core)
    table = [
        (mine, diagonal), (mine, y_up), (mine, y_down), (other_hi, y_up), (other_hi, y_down),
        (own_before, y_up), (other_after, y_down),
        (mine, sibling), (other_hi, sibling), (own_before, sibling), (own_after, sibling),
        (other_before, sibling), (other_after, sibling), (own_far, sibling), (other_far, sibling),
        (own_before, y_up), (own_after, y_down), (own_far, across),
    ]

    def spread(q, no):
        which, device = table[no]
        src = dst = held[q].at[which]
        half = SIZES[q] // 2
        if no == 0:
            src = theirs[q]
        elif no == 15:
            src = dst = held[q].at[which, :, pl.ds(0, half)]
        elif no == 16:
            src = dst = held[q].at[which, :, pl.ds(half, half)]
        return remote(("spread", q, no), src, dst, pass_send.at[q, no], pass_recv.at[q, no], device)

    def ask():
        return remote(("ask",), offsets_ref, beside_offsets, asked_send.at[0], asked_recv.at[0], beside)

    def choose(q):
        for hop in range(5):
            side(hop, q).wait_recv()
        if q == 0:
            ask().wait_recv()
        for slot in range(K):
            offset = beside_offsets[0, slot]
            odd = lax.rem(offset, 2)
            place = offset // 2 + 5 - odd * (4 + x_lo)
            rows = near[q][place]
            theirs[q][slot] = jnp.where(chan + 1 - 2 * x_lo + offset < NB, rows, jnp.zeros_like(rows))
        spread(q, 0).start()
        for slot in range(K):
            offset = offsets_ref[0, slot]
            odd = lax.rem(offset, 2)
            place = offset // 2 + odd * (5 + x_lo)
            rows = near[q][place]
            held[q][mine, slot] = jnp.where(chan + offset < NB, rows, jnp.zeros_like(rows))
        for no in (1, 2, 7):
            spread(q, no).start()

    def other_in(q):
        spread(q, 0).wait_recv()
        for no in (3, 4, 8):
            spread(q, no).start()

    def own_before_in(q):
        spread(q, 1).wait_recv()
        spread(q, 15 if q in TURNED else 5).start()
        spread(q, 9).start()

    def own_after_in(q):
        spread(q, 2).wait_recv()
        if q in TURNED:
            spread(q, 16).start()
        spread(q, 10).start()

    def other_after_in(q):
        spread(q, 4).wait_recv()
        if q not in TURNED:
            spread(q, 6).start()
        spread(q, 12).start()

    def other_before_in(q):
        spread(q, 3).wait_recv()
        spread(q, 11).start()

    def own_far_in(q):
        if q in TURNED:
            spread(q, 15).wait_recv()
            spread(q, 16).wait_recv()
            spread(q, 17).start()
        else:
            spread(q, 5).wait_recv()
        spread(q, 13).start()

    def other_far_in(q):
        spread(q, 17 if q in TURNED else 6).wait_recv()
        spread(q, 14).start()

    def pair_terms(q):
        for no in range(7, 15):
            spread(q, no).wait_recv()

        def group(g, carry):
            at = pl.ds(pl.multiple_of(g * 16, 16), 16)
            right = jnp.concatenate([held[q][:, slot, at, :].reshape(256, BLK) for slot in range(K)], axis=1)
            no = FIRST[q] // 16 + g
            tile = left[
                pl.ds(pl.multiple_of(no // 4 * 128, 128), 128), pl.ds(pl.multiple_of(lax.rem(no, 4) * 256, 256), 256)
            ]
            both = jnp.dot(tile, right, preferred_element_type=F32)
            for slot in range(K):
                terms[q % 2, slot, :, at, :] = both[:, BLK * slot : BLK * (slot + 1)].astype(BF16).reshape(8, 16, BLK)
            return carry

        lax.fori_loop(0, SIZES[q] // 16, group, 0, unroll=4)

    lag_scale = 1.0 / (W * math.sqrt(F))

    def out_copy(m):
        at = pl.ds(m * 4, 4)
        return pltpu.make_async_copy(done.at[at], out_ref.at[at], out_sem.at[m])

    def lag_sums(q, half):
        def lags(m, carry):
            at = pl.ds(m * 4, 4)
            part = jnp.concatenate([terms[q % 2, m // 2, lax.rem(m, 2) * 4 + n, : SIZES[q], :].T for n in range(4)], axis=0)
            part = jnp.dot(part, lag_ref[FIRST[q] : FIRST[q] + SIZES[q], :], preferred_element_type=F32)
            part = part.reshape(4, BLK, LAGS)
            if q > 0:
                part = total[at] + part
            if q < NQ - 1:
                total[at] = part
            else:
                done[at] = (part * lag_scale).astype(BF16)
                out_copy(m).start()
            return carry

        lax.fori_loop(K * half, K * half + K, lags, 0)
        if q == NQ - 1 and half == 1:
            for m in range(K * 2):
                out_copy(m).wait()

    def build_left(v):
        if v == 0:
            for shift in range(1, 16):
                owner_rows(shift).wait_recv()
        lane = lax.broadcasted_iota(jnp.int32, (16, 128), 1)
        row = lax.broadcasted_iota(jnp.int32, (16, 128), 0)
        same_bin = (lane % 16) // 2 == row // 2
        even_row = row % 2 == 0
        slab = lane // 16
        even_lane = lane % 2 == 0

        def step(s, carry):
            for half in range(2):
                got = jnp.zeros((16, 128), F32)
                for w in range(8):
                    part = rows_in[half * 8 + w, :, 128 * v : 128 * v + 128].astype(F32)
                    got = jnp.where(slab == w, pltpu.roll(part, lax.rem(16 * (w + 8 - s), 128), 1), got)
                swapped = jnp.where(even_lane, pltpu.roll(got, 127, 1), -pltpu.roll(got, 1, 1))
                for h in range(2):
                    for i in range(8):
                        r = slice(h * 8 + i, h * 8 + i + 1)
                        value = jnp.where(even_row, got[r], swapped[r])
                        no = h * 32 + v * 8 + s
                        left[
                            pl.ds(pl.multiple_of(no // 4 * 128 + 16 * i, 16), 16),
                            pl.ds(pl.multiple_of(lax.rem(no, 4) * 256 + 128 * half, 128), 128),
                        ] = jnp.where(same_bin, value, 0.0).astype(BF16)
            return carry

        lax.fori_loop(0, 8, step, 0, unroll=2)

    def own_start():
        ask().start()
        for shift in range(1, 16):
            owner_rows(shift).start()

    steps = dict(
        s=begin, w=pass_on, o=own_start, a=choose, b=other_in, c=own_before_in, C=own_after_in, k=other_after_in,
        K=other_before_in, d=own_far_in, h=other_far_in, l=build_left, e=pair_terms, f=lag_sums,
    )
    for item in schedule:
        steps[item[0]](*[int(digit) for digit in item[1:]])
    for key, copy in started.items():
        if key not in waited:
            copy.wait_recv()
        copy.wait_send()

def correlations_of(traces, starts, mask, pair_offsets, basis, lag_basis, schedule=SCHEDULE, name="correlate", collective_id=0):
    dma = pltpu.SemaphoreType.DMA
    return pl.pallas_call(
        functools.partial(correlate_kernel, schedule),
        name=name,
        out_shape=jax.ShapeDtypeStruct((K * 8, BLK, LAGS), BF16),
        in_specs=[pl.BlockSpec(memory_space=pl.ANY)] * 6,
        out_specs=pl.BlockSpec(memory_space=pl.ANY),
        scratch_shapes=[pltpu.VMEM((10, size, BLK), BF16) for size in SIZES]
        + [pltpu.VMEM((16, K, size, BLK), BF16) for size in SIZES]
        + [pltpu.VMEM((K, size, BLK), BF16) for size in SIZES]
        + [
            pltpu.VMEM((16, 16, F), BF16),
            pltpu.VMEM((16, 16, F), BF16),
            pltpu.VMEM((L, ROWS), BF16),
            pltpu.VMEM((2, K, 8, max(SIZES), BLK), BF16),
            pltpu.VMEM((K * 8, BLK, LAGS), F32),
            pltpu.VMEM((K * 8, BLK, LAGS), BF16),
            dma((K * 2,)),
            pltpu.SMEM((1,), jnp.int32),
            pltpu.VMEM((BLK, SEG), BF16),
            pltpu.VMEM((1, BLK), jnp.int32),
            pltpu.SMEM((1, K), jnp.int32),
            pltpu.SMEM((1, K), jnp.int32),
            pltpu.VMEM((ROWS, LAGS), BF16),
            dma((6,)), dma((1,)), dma((1,)),
            dma((NQ, 4)), dma((NQ, 4)), dma((NQ, 5)), dma((NQ, 5)),
            dma((15,)), dma((15,)), dma((NQ, 18)), dma((NQ, 18)),
        ],
        compiler_params=pltpu.CompilerParams(
            collective_id=collective_id, has_side_effects=True, vmem_limit_bytes=VMEM_MIB * 2**20
        ),
    )(starts, traces, mask.reshape(1, BLK), pair_offsets, basis, lag_basis)


def deliver_kernel(src_ref, dst_ref, held, in_sem, out_sem):
    count = in_sem.shape[0]
    size = src_ref.shape[0] // count
    parts = [pl.ds(size * n, size) for n in range(count)]
    ins = [pltpu.make_async_copy(src_ref.at[p], held.at[p], in_sem.at[n]) for n, p in enumerate(parts)]
    outs = [pltpu.make_async_copy(held.at[p], dst_ref.at[p], out_sem.at[n]) for n, p in enumerate(parts)]
    for copy in ins:
        copy.start()
    for copy_in, copy_out in zip(ins, outs):
        copy_in.wait()
        copy_out.start()
    for copy in outs:
        copy.wait()


def on_device(traces, starts, mask, pair_offsets):
    out = correlations_of(traces, starts, mask, pair_offsets, jnp.asarray(dft_table()), jnp.asarray(lag_table()))
    out = pl.pallas_call(
        deliver_kernel,
        name="deliver",
        out_shape=jax.ShapeDtypeStruct(out.shape, BF16),
        in_specs=[pl.BlockSpec(memory_space=pl.ANY)],
        out_specs=pl.BlockSpec(memory_space=pl.ANY),
        scratch_shapes=[pltpu.VMEM(out.shape, BF16), pltpu.SemaphoreType.DMA((4,)), pltpu.SemaphoreType.DMA((4,))],
        compiler_params=pltpu.CompilerParams(vmem_limit_bytes=VMEM_MIB * 2**20),
    )(out)
    return out.reshape(1, K, 8, BLK, LAGS)


def solution(mesh):
    in_specs = (P("chan", "freq"), P("freq"), P("chan"), P("chan", None))
    out_specs = P("chan", None, "freq", None, None)
    return jax.shard_map(
        on_device, mesh=mesh, in_specs=in_specs, out_specs=out_specs, check_vma=False
    )
```

time: 119 us -> 92.5 us (0.78)
  matrix products: 11.4 us -> 0 us
  Pallas kernels: 102 us -> 91.7 us
  local copies, waits for them, and re-layouts: 4.66 us -> 0 us
    dot_general x1 -> x0, matrix products: 11.4 us -> none  [on_device(): jnp.dot(pair_spectra.reshape(K * 8 * BLK, ROWS), jnp.asarray(lag_table())...]
    pallas_call x2, Pallas kernels: 102 us -> 91.7 us  [the longest x1 86.6 us: correlations_of(): pl.pallas_call(functools.partial(correlate_kernel, schedule), name=name,...]
    unnamed x8 -> x0, local copies, waits for them, and re-layouts: 3.9 us -> none
where the time goes in v2:
time: 92.5 us; the launch traced here: 92.4 us
  Pallas kernels  91.7 us (99%)
    pallas_call x1, Pallas kernels, correlations_of(): pl.pallas_call(functools.partial(correlate_kernel, schedule), name=name,...  86.6 us
    pallas_call x1, Pallas kernels, on_device(): pl.pallas_call(deliver_kernel, name='deliver', out_shape=jax.ShapeDtypeSt...  5.16 us

profile of v2, /device:TPU:1, one launch (start us, length us, event | category | flops | bytes accessed | tf_op | source)
XLA Modules:
  0.0 92.4 jit_solution(7818712924863662197)
XLA Ops:
  0.7 86.6 %correlate.1.src_ref = bf16[24,128,1024]{2,1,0:T(8,128)(2,1)} custom-call(s32[1]{0:T(128)S(6)} %copy.7.starts_hbm, bf16[128,2304]{1,0:T(8,128)(2,1)} %traces_hbm.1, s32[1,128]{1,0:T(1,128)} %bitcast.2, s32[1,3]{1,0:T(1,128)} %offsets_hbm.1, bf16[2048,1024]{1,0:T(8,128)(2,1)} %constant.4.clone.basis_hbm, bf16[1024,1024]{1,0:T(8,128)(2,1)} %constant.5.clone.lag_hbm), custom_call_target="tpu_custom_call" | custom-call | tf_op jit(solution)/shard_map/correlate/pallas_call | solution.py:347
  87.2 5.2 %deliver.1 = bf16[24,128,1024]{2,1,0:T(8,128)(2,1)} custom-call(bf16[24,128,1024]{2,1,0:T(8,128)(2,1)} %correlate.1.src_ref), custom_call_target="tpu_custom_call" | custom-call | tf_op jit(solution)/shard_map/deliver/pallas_call | solution.py:397

commit v3 on v2

--- a/solution.py
+++ b/solution.py
@@ -20,10 +20,10 @@
 LAGS = 1024
 K = 3
 ROWS = 2 * F
-SIZES = (128, 128, 192, 192, 192, 192)
+SIZES = (128, 128, 64, 192, 256, 128, 128)
 NQ = len(SIZES)
 FIRST = tuple(sum(SIZES[:q]) for q in range(NQ))
-TURNED = (0, 1, 2, 3)
+TURNED = (0, 1, 2, 3, 4)
 VMEM_MIB = 60
 MESH = pl.DeviceIdType.MESH
 BF16 = jnp.bfloat16
@@ -60,32 +60,39 @@
         self.waited.add(self.key)
 
 
+GROUPS = ((0, 3), (3, 5), (5, 7))
+GROUP_ROWS = tuple(sum(SIZES[first:end]) for first, end in GROUPS)
+LATE = GROUP_ROWS[-1]
+
 SCHEDULE = (
-    "s0", "o", "w10", "s1", "w20", "l0", "w11", "s2", "l1", "w30", "l2", "w21", "l3", "w12", "s3", "w40", "w31",
-    "w22", "w13", "s4", "a0", "w41", "w32", "w23", "w14", "s5", "a1", "b0", "c0", "C0", "w42", "w33", "w24",
-    "w15", "b1", "c1", "C1", "w43", "a2", "w34", "k0", "K0", "w25", "d0", "a3", "w44", "k1", "K1", "w35", "d1",
-    "b2", "w45", "h0", "c2", "C2", "a4", "e0", "f00", "b3", "c3", "C3", "f01", "h1", "a5", "k2", "K2", "e1",
-    "f10", "b4", "d2", "f11", "c4", "C4", "b5", "k3", "K3", "h2", "d3", "e2", "f20", "c5", "C5", "f21", "h3",
-    "k4", "K4", "e3", "f30", "d4", "k5", "f31", "h4", "K5", "e4", "f40", "d5", "h5", "f41", "e5", "f50", "f51",
+    "s0", "s1", "o", "w10", "s2", "w11", "s3", "w20", "l0", "w12", "w21", "s4", "l1", "w13", "w30", "s5", "l2",
+    "w22", "w31", "l3", "w14", "s6", "w23", "w40", "a0", "w15", "w32", "w41", "a1", "w24", "w16", "b0", "c0",
+    "C0", "w33", "w25", "w42", "a2", "b1", "c1", "C1", "w34", "w26", "k0", "K0", "w43", "d0", "b2", "a3", "w35",
+    "c2", "C2", "w44", "k1", "K1", "d1", "a4", "w36", "w45", "k2", "K2", "h0", "e0", "c3", "C3", "a5", "w46",
+    "d2", "b3", "h1", "c4", "C4", "e1", "a6", "d3", "b4", "c5", "C5", "b5", "h2", "k3", "K3", "e2", "b6", "f00",
+    "d4", "f01", "c6", "C6", "h3", "e3", "k4", "K4", "h4", "k5", "d5", "e4", "K5", "k6", "f10", "K6", "h5", "f11",
+    "d6", "e5", "h6", "e6",
 )
 
 
 def correlate_kernel(
-    schedule, starts_hbm, traces_hbm, mask_hbm, offsets_hbm, basis_hbm, lag_hbm, out_ref,
+    schedule, starts_hbm, traces_hbm, mask_hbm, offsets_hbm, basis_hbm, lag_hbm, sums_ref, late_ref,
     *scratch,
 ):
     near = scratch[:NQ]
     held = scratch[NQ : 2 * NQ]
     theirs = scratch[2 * NQ : 3 * NQ]
+    terms = scratch[3 * NQ : 3 * NQ + len(GROUPS)]
     (
-        by_owner, rows_in, left, terms, total, done, out_sem,
+        by_owner, rows_in, left, total, done, out_sem, late_sem,
         starts_ref, traces_ref, mask_ref, offsets_ref, beside_offsets, lag_ref, load_sem, asked_send, asked_recv,
         chain_send, chain_recv, side_send, side_recv, own_send, own_recv, pass_send, pass_recv,
-    ) = scratch[3 * NQ :]
+    ) = scratch[3 * NQ + len(GROUPS) :]
     basis_ref = left
+    parts = [slice(n * 512, n * 512 + 512) for n in range(4)]
     operands = [
-        (starts_hbm, starts_ref), (traces_hbm, traces_ref), (mask_hbm, mask_ref),
-        (basis_hbm, basis_ref), (offsets_hbm, offsets_ref), (lag_hbm, lag_ref),
+        (starts_hbm, starts_ref), (traces_hbm, traces_ref), *[(basis_hbm.at[p], basis_ref.at[p]) for p in parts],
+        (mask_hbm, mask_ref), (offsets_hbm, offsets_ref), (lag_hbm, lag_ref),
     ]
     loads = [pltpu.make_async_copy(src, dst, load_sem.at[no]) for no, (src, dst) in enumerate(operands)]
     for load in loads:
@@ -105,6 +112,8 @@
     beside = (chan + 1 - 2 * x_lo, freq)
     sibling = (chan, window(x_hi, y, 1 - core))
     across = (chan, window(1 - x_hi, y, core))
+    below_beside = (lax.rem(chan + 14, 16) + 1 - 2 * x_lo, freq)
+    above_beside = (lax.rem(chan + 2, 16) + 1 - 2 * x_lo, freq)
     diagonal = (chan + 1 - 2 * x_lo, window(1 - x_hi, y, core))
     y_up = (chan, window(x_hi, y + 1, core))
     y_down = (chan, window(x_hi, y + 3, core))
@@ -112,13 +121,19 @@
 
     started, waited = {}, set()
     barrier = pltpu.get_barrier_semaphore()
-    everyone = peers + [below, above, beside, diagonal]
+    everyone = peers + [below, above, beside, diagonal, below_beside, above_beside]
     for other in everyone:
         pl.semaphore_signal(barrier, inc=1, device_id=other, device_id_type=MESH)
-    for load in loads[:4]:
+    loads[0].wait()
+    loads[1].wait()
+    shifted = pltpu.roll(traces_ref[...].astype(F32), lax.rem(SEG - starts_ref[0], SEG), 1)
+    segment = shifted[:, :L].astype(BF16)
+    spectra = jnp.zeros((BLK, ROWS), F32)
+    for n, p in enumerate(parts):
+        loads[2 + n].wait()
+        spectra = spectra + jnp.dot(segment[:, p], basis_ref[p, :], preferred_element_type=F32)
+    for load in loads[6:]:
         load.wait()
-    shifted = pltpu.roll(traces_ref[...].astype(F32), lax.rem(SEG - starts_ref[0], SEG), 1)
-    spectra = jnp.dot(shifted[:, :L].astype(BF16), basis_ref[...], preferred_element_type=F32)
     power_mean = jnp.sum(spectra * spectra, axis=1, keepdims=True) / F
     working = jnp.broadcast_to(mask_ref[...].astype(F32), (BLK, BLK)).T[:, :1]
     whitened = spectra * (lax.rsqrt(power_mean + 1e-06) * working)
@@ -129,8 +144,6 @@
         rows = whitened[8 * owner : 8 * owner + 8]
         by_owner[owner] = jnp.concatenate([rows[:, :F], rows[:, F:]], axis=0).astype(BF16)
     rows_in[freq] = by_owner[freq]
-    loads[4].wait()
-    loads[5].wait()
     pl.semaphore_wait(barrier, len(everyone))
 
     def remote(key, src, dst, send, recv, device):
@@ -143,7 +156,8 @@
         return remote(("chain", hop, q), near[q].at[hop - 1], near[q].at[hop], chain_send.at[q, hop - 1], chain_recv.at[q, hop - 1], below)
 
     def side(hop, q):
-        return remote(("side", hop, q), near[q].at[hop], near[q].at[5 + hop], side_send.at[q, hop], side_recv.at[q, hop], beside)
+        src, device = (hop, beside) if hop < 4 else (3, below_beside)
+        return remote(("side", hop, q), near[q].at[src], near[q].at[5 + hop], side_send.at[q, hop], side_recv.at[q, hop], device)
 
     def owner_rows(shift):
         there = lax.rem(freq + shift, 16)
@@ -157,7 +171,9 @@
         chain(hop, q).wait_recv()
         if hop < 4:
             chain(hop + 1, q).start()
-        side(hop, q).start()
+            side(hop, q).start()
+        if hop == 3:
+            side(4, q).start()
 
     mine = window(x_hi, y, core)
     other_hi = window(1 - x_hi, y, core)
@@ -251,49 +267,59 @@
         spread(q, 17 if q in TURNED else 6).wait_recv()
         spread(q, 14).start()
 
+    def group_of(q):
+        no = [first <= q < end for first, end in GROUPS].index(True)
+        return no, FIRST[q] - FIRST[GROUPS[no][0]]
+
+    def late_copy(q):
+        rows = pl.ds(group_of(q)[1], SIZES[q])
+        return pltpu.make_async_copy(terms[-1].at[:, :, rows], late_ref.at[:, :, rows], late_sem.at[NQ - 1 - q])
+
     def pair_terms(q):
+        which, base = group_of(q)
+
         for no in range(7, 15):
             spread(q, no).wait_recv()
 
         def group(g, carry):
             at = pl.ds(pl.multiple_of(g * 16, 16), 16)
             right = jnp.concatenate([held[q][:, slot, at, :].reshape(256, BLK) for slot in range(K)], axis=1)
+            to = pl.ds(pl.multiple_of(base + g * 16, 16), 16)
             no = FIRST[q] // 16 + g
             tile = left[
                 pl.ds(pl.multiple_of(no // 4 * 128, 128), 128), pl.ds(pl.multiple_of(lax.rem(no, 4) * 256, 256), 256)
             ]
             both = jnp.dot(tile, right, preferred_element_type=F32)
             for slot in range(K):
-                terms[q % 2, slot, :, at, :] = both[:, BLK * slot : BLK * (slot + 1)].astype(BF16).reshape(8, 16, BLK)
+                terms[which][slot, :, to, :] = both[:, BLK * slot : BLK * (slot + 1)].astype(BF16).reshape(8, 16, BLK)
             return carry
 
         lax.fori_loop(0, SIZES[q] // 16, group, 0, unroll=4)
-
-    lag_scale = 1.0 / (W * math.sqrt(F))
-
-    def out_copy(m):
+        if which == len(GROUPS) - 1:
+            late_copy(q).start()
+
+    def sums_copy(m):
         at = pl.ds(m * 4, 4)
-        return pltpu.make_async_copy(done.at[at], out_ref.at[at], out_sem.at[m])
-
-    def lag_sums(q, half):
+        return pltpu.make_async_copy(done.at[at], sums_ref.at[at], out_sem.at[m])
+
+    def lag_sums(which, half):
+        first = FIRST[GROUPS[which][0]]
+
         def lags(m, carry):
             at = pl.ds(m * 4, 4)
-            part = jnp.concatenate([terms[q % 2, m // 2, lax.rem(m, 2) * 4 + n, : SIZES[q], :].T for n in range(4)], axis=0)
-            part = jnp.dot(part, lag_ref[FIRST[q] : FIRST[q] + SIZES[q], :], preferred_element_type=F32)
+            part = jnp.concatenate([terms[which][m // 2, lax.rem(m, 2) * 4 + n].T for n in range(4)], axis=0)
+            part = jnp.dot(part, lag_ref[first : first + GROUP_ROWS[which], :], preferred_element_type=F32)
             part = part.reshape(4, BLK, LAGS)
-            if q > 0:
+            if which > 0:
                 part = total[at] + part
-            if q < NQ - 1:
+            if which < len(GROUPS) - 2:
                 total[at] = part
             else:
-                done[at] = (part * lag_scale).astype(BF16)
-                out_copy(m).start()
+                done[at] = part.astype(BF16)
+                sums_copy(m).start()
             return carry
 
         lax.fori_loop(K * half, K * half + K, lags, 0)
-        if q == NQ - 1 and half == 1:
-            for m in range(K * 2):
-                out_copy(m).wait()
 
     def build_left(v):
         if v == 0:
@@ -337,6 +363,10 @@
     )
     for item in schedule:
         steps[item[0]](*[int(digit) for digit in item[1:]])
+    for m in range(K * 2):
+        sums_copy(m).wait()
+    for q in range(*GROUPS[-1]):
+        late_copy(q).wait()
     for key, copy in started.items():
         if key not in waited:
             copy.wait_recv()
@@ -347,27 +377,31 @@
     return pl.pallas_call(
         functools.partial(correlate_kernel, schedule),
         name=name,
-        out_shape=jax.ShapeDtypeStruct((K * 8, BLK, LAGS), BF16),
+        out_shape=(
+            jax.ShapeDtypeStruct((K * 8, BLK, LAGS), BF16),
+            jax.ShapeDtypeStruct((K, 8, LATE, BLK), BF16),
+        ),
         in_specs=[pl.BlockSpec(memory_space=pl.ANY)] * 6,
-        out_specs=pl.BlockSpec(memory_space=pl.ANY),
+        out_specs=(pl.BlockSpec(memory_space=pl.ANY), pl.BlockSpec(memory_space=pl.ANY)),
         scratch_shapes=[pltpu.VMEM((10, size, BLK), BF16) for size in SIZES]
         + [pltpu.VMEM((16, K, size, BLK), BF16) for size in SIZES]
         + [pltpu.VMEM((K, size, BLK), BF16) for size in SIZES]
+        + [pltpu.VMEM((K, 8, rows, BLK), BF16) for rows in GROUP_ROWS]
         + [
             pltpu.VMEM((16, 16, F), BF16),
             pltpu.VMEM((16, 16, F), BF16),
             pltpu.VMEM((L, ROWS), BF16),
-            pltpu.VMEM((2, K, 8, max(SIZES), BLK), BF16),
             pltpu.VMEM((K * 8, BLK, LAGS), F32),
             pltpu.VMEM((K * 8, BLK, LAGS), BF16),
             dma((K * 2,)),
+            dma((GROUPS[-1][1] - GROUPS[-1][0],)),
             pltpu.SMEM((1,), jnp.int32),
             pltpu.VMEM((BLK, SEG), BF16),
             pltpu.VMEM((1, BLK), jnp.int32),
             pltpu.SMEM((1, K), jnp.int32),
             pltpu.SMEM((1, K), jnp.int32),
             pltpu.VMEM((ROWS, LAGS), BF16),
-            dma((6,)), dma((1,)), dma((1,)),
+            dma((9,)), dma((1,)), dma((1,)),
             dma((NQ, 4)), dma((NQ, 4)), dma((NQ, 5)), dma((NQ, 5)),
             dma((15,)), dma((15,)), dma((NQ, 18)), dma((NQ, 18)),
         ],
@@ -377,32 +411,51 @@
     )(starts, traces, mask.reshape(1, BLK), pair_offsets, basis, lag_basis)
 
 
-def deliver_kernel(src_ref, dst_ref, held, in_sem, out_sem):
-    count = in_sem.shape[0]
-    size = src_ref.shape[0] // count
-    parts = [pl.ds(size * n, size) for n in range(count)]
-    ins = [pltpu.make_async_copy(src_ref.at[p], held.at[p], in_sem.at[n]) for n, p in enumerate(parts)]
-    outs = [pltpu.make_async_copy(held.at[p], dst_ref.at[p], out_sem.at[n]) for n, p in enumerate(parts)]
-    for copy in ins:
-        copy.start()
-    for copy_in, copy_out in zip(ins, outs):
-        copy_in.wait()
-        copy_out.start()
+def finish_kernel(sums_hbm, late_hbm, lag_hbm, out_hbm, sums, late, lag, done, lag_sem, late_sem, sums_sem, out_sem):
+    chunks = [pl.ds(m * 4, 4) for m in range(K * 2)]
+    lag_in = pltpu.make_async_copy(lag_hbm.at[pl.ds(ROWS - LATE, LATE)], lag, lag_sem.at[0])
+    late_in = [pltpu.make_async_copy(late_hbm.at[at], late.at[at], late_sem.at[m]) for m, at in enumerate(chunks)]
+    sums_in = [pltpu.make_async_copy(sums_hbm.at[at], sums.at[at], sums_sem.at[m]) for m, at in enumerate(chunks)]
+    outs = [pltpu.make_async_copy(done.at[at], out_hbm.at[at], out_sem.at[m]) for m, at in enumerate(chunks)]
+    lag_in.start()
+    for m in range(2):
+        late_in[m].start()
+        sums_in[m].start()
+    lag_in.wait()
+    lag_scale = 1.0 / (W * math.sqrt(F))
+    for m, at in enumerate(chunks):
+        late_in[m].wait()
+        sums_in[m].wait()
+        if m + 2 < K * 2:
+            late_in[m + 2].start()
+            sums_in[m + 2].start()
+        part = jnp.concatenate([late[4 * m + n].T for n in range(4)], axis=0)
+        part = jnp.dot(part, lag[...], preferred_element_type=F32).reshape(4, BLK, LAGS)
+        done[at] = ((sums[at].astype(F32) + part) * lag_scale).astype(BF16)
+        outs[m].start()
     for copy in outs:
         copy.wait()
 
 
 def on_device(traces, starts, mask, pair_offsets):
-    out = correlations_of(traces, starts, mask, pair_offsets, jnp.asarray(dft_table()), jnp.asarray(lag_table()))
+    lag_basis = jnp.asarray(lag_table())
+    sums, late = correlations_of(traces, starts, mask, pair_offsets, jnp.asarray(dft_table()), lag_basis)
+    dma = pltpu.SemaphoreType.DMA
     out = pl.pallas_call(
-        deliver_kernel,
-        name="deliver",
-        out_shape=jax.ShapeDtypeStruct(out.shape, BF16),
-        in_specs=[pl.BlockSpec(memory_space=pl.ANY)],
+        finish_kernel,
+        name="finish",
+        out_shape=jax.ShapeDtypeStruct((K * 8, BLK, LAGS), BF16),
+        in_specs=[pl.BlockSpec(memory_space=pl.ANY)] * 3,
         out_specs=pl.BlockSpec(memory_space=pl.ANY),
-        scratch_shapes=[pltpu.VMEM(out.shape, BF16), pltpu.SemaphoreType.DMA((4,)), pltpu.SemaphoreType.DMA((4,))],
+        scratch_shapes=[
+            pltpu.VMEM((K * 8, BLK, LAGS), BF16),
+            pltpu.VMEM((K * 8, LATE, BLK), BF16),
+            pltpu.VMEM((LATE, LAGS), BF16),
+            pltpu.VMEM((K * 8, BLK, LAGS), BF16),
+            dma((1,)), dma((K * 2,)), dma((K * 2,)), dma((K * 2,)),
+        ],
         compiler_params=pltpu.CompilerParams(vmem_limit_bytes=VMEM_MIB * 2**20),
-    )(out)
+    )(sums, late.reshape(K * 8, LATE, BLK), lag_basis)
     return out.reshape(1, K, 8, BLK, LAGS)
 
 

time: 92.5 us -> 89.6 us (0.969)
  Pallas kernels: 91.7 us -> 88.8 us
    pallas_call x1, Pallas kernels: 86.6 us -> 81.7 us  [correlations_of(): pl.pallas_call(functools.partial(correlate_kernel, schedule), name=name,...]
    pallas_call x1, Pallas kernels: 5.16 us -> 7.05 us  [on_device(): pl.pallas_call(finish_kernel, name='finish', out_shape=jax.ShapeDtypeStru...]
where the time goes in v3:
time: 89.6 us; the launch traced here: 89.4 us
  Pallas kernels  88.8 us (99%)
    pallas_call x1, Pallas kernels, correlations_of(): pl.pallas_call(functools.partial(correlate_kernel, schedule), name=name,...  81.7 us
    pallas_call x1, Pallas kernels, on_device(): pl.pallas_call(finish_kernel, name='finish', out_shape=jax.ShapeDtypeStru...  7.05 us

profile of v3, /device:TPU:1, one launch (start us, length us, event | category | flops | bytes accessed | tf_op | source)
XLA Modules:
  0.0 89.4 jit_solution(15786149112180963299)
XLA Ops:
  0.7 81.7 %correlate.1 = (bf16[24,128,1024]{2,1,0:T(8,128)(2,1)}, bf16[3,8,256,128]{3,2,1,0:T(8,128)(2,1)}) custom-call(s32[1]{0:T(128)S(6)} %copy.7.starts_hbm, bf16[128,2304]{1,0:T(8,128)(2,1)} %traces_hbm.1, s32[1,128]{1,0:T(1,128)} %bitcast.4, s32[1,3]{1,0:T(1,128)} %offsets_hbm.1, bf16[2048,1024]{1,0:T(8,128)(2,1)} %constant.5.clone.basis_hbm, ...), custom_call_target="tpu_custom_call" | custom-call | tf_op jit(solution)/shard_map/correlate/pallas_call | solution.py:377
  82.4 7.0 %finish.1 = bf16[24,128,1024]{2,1,0:T(8,128)(2,1)} custom-call(bf16[24,128,1024]{2,1,0:T(8,128)(2,1)} %get-tuple-element.7.sums_hbm, bf16[24,256,128]{2,1,0:T(8,128)(2,1)} %bitcast.3, bf16[1024,1024]{1,0:T(8,128)(2,1)} %constant.4.clone.lag_hbm), custom_call_target="tpu_custom_call" | custom-call | tf_op jit(solution)/shard_map/finish/pallas_call | solution.py:444

commit v4 on v3

--- a/solution.py
+++ b/solution.py
@@ -20,7 +20,7 @@
 LAGS = 1024
 K = 3
 ROWS = 2 * F
-SIZES = (128, 128, 64, 192, 256, 128, 128)
+SIZES = (128, 128, 256, 64, 128, 192, 128)
 NQ = len(SIZES)
 FIRST = tuple(sum(SIZES[:q]) for q in range(NQ))
 TURNED = (0, 1, 2, 3, 4)
@@ -65,13 +65,13 @@
 LATE = GROUP_ROWS[-1]
 
 SCHEDULE = (
-    "s0", "s1", "o", "w10", "s2", "w11", "s3", "w20", "l0", "w12", "w21", "s4", "l1", "w13", "w30", "s5", "l2",
-    "w22", "w31", "l3", "w14", "s6", "w23", "w40", "a0", "w15", "w32", "w41", "a1", "w24", "w16", "b0", "c0",
-    "C0", "w33", "w25", "w42", "a2", "b1", "c1", "C1", "w34", "w26", "k0", "K0", "w43", "d0", "b2", "a3", "w35",
-    "c2", "C2", "w44", "k1", "K1", "d1", "a4", "w36", "w45", "k2", "K2", "h0", "e0", "c3", "C3", "a5", "w46",
-    "d2", "b3", "h1", "c4", "C4", "e1", "a6", "d3", "b4", "c5", "C5", "b5", "h2", "k3", "K3", "e2", "b6", "f00",
-    "d4", "f01", "c6", "C6", "h3", "e3", "k4", "K4", "h4", "k5", "d5", "e4", "K5", "k6", "f10", "K6", "h5", "f11",
-    "d6", "e5", "h6", "e6",
+    "s0", "o", "w10", "s1", "w20", "l0", "w11", "s2", "l1", "w30", "l2", "w21", "l3", "w12", "s3", "w40", "a0",
+    "w31", "w22", "w13", "s4", "w41", "b0", "c0", "C0", "a1", "w32", "w23", "w14", "s5", "k0", "K0", "w42", "b1",
+    "d0", "w33", "a2", "w24", "c1", "C1", "w15", "s6", "w43", "k1", "K1", "h0", "a3", "w34", "e0", "w25", "w16",
+    "c2", "C2", "b2", "d1", "w44", "b3", "c3", "C3", "a4", "w35", "w26", "d2", "h1", "w45", "e1", "b4", "a5",
+    "w36", "K2", "k2", "K3", "k3", "d3", "c4", "C4", "w46", "h2", "K4", "k4", "a6", "e2", "b5", "c5", "h3", "C5",
+    "f00", "d4", "e3", "b6", "f01", "c6", "C6", "f02", "K5", "k5", "h4", "e4", "k6", "d5", "f10", "f11", "K6",
+    "f12", "h5", "d6", "h6", "e5", "e6",
 )
 
 
@@ -137,13 +137,11 @@
     power_mean = jnp.sum(spectra * spectra, axis=1, keepdims=True) / F
     working = jnp.broadcast_to(mask_ref[...].astype(F32), (BLK, BLK)).T[:, :1]
     whitened = spectra * (lax.rsqrt(power_mean + 1e-06) * working)
-    by_bin = whitened.T.astype(BF16)
-    for q in range(NQ):
-        near[q][0] = by_bin[FIRST[q] : FIRST[q] + SIZES[q], :]
-    for owner in range(16):
-        rows = whitened[8 * owner : 8 * owner + 8]
-        by_owner[owner] = jnp.concatenate([rows[:, :F], rows[:, F:]], axis=0).astype(BF16)
-    rows_in[freq] = by_owner[freq]
+    def turn_piece(q):
+        near[q][0] = whitened[:, FIRST[q] : FIRST[q] + SIZES[q]].T.astype(BF16)
+
+    for q in range(2):
+        turn_piece(q)
     pl.semaphore_wait(barrier, len(everyone))
 
     def remote(key, src, dst, send, recv, device):
@@ -164,6 +162,8 @@
         return remote(("own", shift), by_owner.at[there], rows_in.at[freq], own_send.at[shift - 1], own_recv.at[shift - 1], (chan, there))
 
     def begin(q):
+        if q >= 2:
+            turn_piece(q)
         chain(1, q).start()
         side(0, q).start()
 
@@ -302,7 +302,7 @@
         at = pl.ds(m * 4, 4)
         return pltpu.make_async_copy(done.at[at], sums_ref.at[at], out_sem.at[m])
 
-    def lag_sums(which, half):
+    def lag_sums(which, part_no):
         first = FIRST[GROUPS[which][0]]
 
         def lags(m, carry):
@@ -319,7 +319,7 @@
                 sums_copy(m).start()
             return carry
 
-        lax.fori_loop(K * half, K * half + K, lags, 0)
+        lax.fori_loop(2 * part_no, 2 * part_no + 2, lags, 0)
 
     def build_left(v):
         if v == 0:
@@ -353,6 +353,10 @@
         lax.fori_loop(0, 8, step, 0, unroll=2)
 
     def own_start():
+        for owner in range(16):
+            rows = whitened[8 * owner : 8 * owner + 8]
+            by_owner[owner] = jnp.concatenate([rows[:, :F], rows[:, F:]], axis=0).astype(BF16)
+        rows_in[freq] = by_owner[freq]
         ask().start()
         for shift in range(1, 16):
             owner_rows(shift).start()

time: 89.6 us -> 88.9 us (level)
    pallas_call x1, Pallas kernels: 81.7 us -> 80.4 us  [correlations_of(): pl.pallas_call(functools.partial(correlate_kernel, schedule), name=name,...]
where the time goes in v4:
time: 88.9 us; the launch traced here: 88.7 us
  Pallas kernels  88 us (99%)
    pallas_call x1, Pallas kernels, correlations_of(): pl.pallas_call(functools.partial(correlate_kernel, schedule), name=name,...  80.4 us
    pallas_call x1, Pallas kernels, on_device(): pl.pallas_call(finish_kernel, name='finish', out_shape=jax.ShapeDtypeStru...  7.61 us

profile of v4, /device:TPU:1, one launch (start us, length us, event | category | flops | bytes accessed | tf_op | source)
XLA Modules:
  0.0 88.7 jit_solution(16203873094495358729)
XLA Ops:
  0.7 80.4 %correlate.1 = (bf16[24,128,1024]{2,1,0:T(8,128)(2,1)}, bf16[3,8,320,128]{3,2,1,0:T(8,128)(2,1)}) custom-call(s32[1]{0:T(128)S(6)} %copy.7.starts_hbm, bf16[128,2304]{1,0:T(8,128)(2,1)} %traces_hbm.1, s32[1,128]{1,0:T(1,128)} %bitcast.4, s32[1,3]{1,0:T(1,128)} %offsets_hbm.1, bf16[2048,1024]{1,0:T(8,128)(2,1)} %constant.5.clone.basis_hbm, ...), custom_call_target="tpu_custom_call" | custom-call | tf_op jit(solution)/shard_map/correlate/pallas_call | solution.py:381
  81.1 7.6 %finish.1 = bf16[24,128,1024]{2,1,0:T(8,128)(2,1)} custom-call(bf16[24,128,1024]{2,1,0:T(8,128)(2,1)} %get-tuple-element.7.sums_hbm, bf16[24,320,128]{2,1,0:T(8,128)(2,1)} %bitcast.3, bf16[1024,1024]{1,0:T(8,128)(2,1)} %constant.4.clone.lag_hbm), custom_call_target="tpu_custom_call" | custom-call | tf_op jit(solution)/shard_map/finish/pallas_call | solution.py:448

commit v5 on v4

--- a/solution.py
+++ b/solution.py
@@ -20,7 +20,7 @@
 LAGS = 1024
 K = 3
 ROWS = 2 * F
-SIZES = (128, 128, 256, 64, 128, 192, 128)
+SIZES = (128, 192, 192, 64, 192, 128, 128)
 NQ = len(SIZES)
 FIRST = tuple(sum(SIZES[:q]) for q in range(NQ))
 TURNED = (0, 1, 2, 3, 4)
@@ -65,13 +65,13 @@
 LATE = GROUP_ROWS[-1]
 
 SCHEDULE = (
-    "s0", "o", "w10", "s1", "w20", "l0", "w11", "s2", "l1", "w30", "l2", "w21", "l3", "w12", "s3", "w40", "a0",
-    "w31", "w22", "w13", "s4", "w41", "b0", "c0", "C0", "a1", "w32", "w23", "w14", "s5", "k0", "K0", "w42", "b1",
-    "d0", "w33", "a2", "w24", "c1", "C1", "w15", "s6", "w43", "k1", "K1", "h0", "a3", "w34", "e0", "w25", "w16",
-    "c2", "C2", "b2", "d1", "w44", "b3", "c3", "C3", "a4", "w35", "w26", "d2", "h1", "w45", "e1", "b4", "a5",
-    "w36", "K2", "k2", "K3", "k3", "d3", "c4", "C4", "w46", "h2", "K4", "k4", "a6", "e2", "b5", "c5", "h3", "C5",
-    "f00", "d4", "e3", "b6", "f01", "c6", "C6", "f02", "K5", "k5", "h4", "e4", "k6", "d5", "f10", "f11", "K6",
-    "f12", "h5", "d6", "h6", "e5", "e6",
+    "s0", "o", "w10", "s1", "w20", "l0", "w11", "s2", "l1", "w30", "l2", "l3", "w21", "w12", "s3", "w40", "a0",
+    "w31", "w22", "w13", "s4", "b0", "c0", "C0", "w41", "a1", "w32", "w23", "w14", "s5", "k0", "K0", "d0", "w42",
+    "w33", "a2", "b1", "w24", "c1", "C1", "w15", "s6", "w43", "h0", "a3", "w34", "e0", "c2", "C2", "w25", "w16",
+    "b2", "b3", "w44", "k1", "K1", "a4", "w35", "d1", "w26", "c3", "C3", "d2", "w45", "a5", "w36", "b4", "k2",
+    "K2", "k3", "K3", "w46", "h1", "c4", "C4", "d3", "e1", "c5", "C5", "h2", "a6", "b5", "e2", "k4", "K4", "h3",
+    "d4", "f00", "f01", "d5", "b6", "C6", "e3", "f02", "c6", "k5", "h4", "K5", "e4", "k6", "K6", "f10", "h5",
+    "f11", "d6", "f12", "e5", "h6", "e6",
 )
 
 

time: 88.9 us -> 88.1 us (level)
  no operation moved by 1% of the time
where the time goes in v5:
time: 88.1 us; the launch traced here: 87.9 us
  Pallas kernels  87.2 us (99%)
    pallas_call x1, Pallas kernels, correlations_of(): pl.pallas_call(functools.partial(correlate_kernel, schedule), name=name,...  80.2 us
    pallas_call x1, Pallas kernels, on_device(): pl.pallas_call(finish_kernel, name='finish', out_shape=jax.ShapeDtypeStru...  7.05 us

profile of v5, /device:TPU:1, one launch (start us, length us, event | category | flops | bytes accessed | tf_op | source)
XLA Modules:
  0.0 87.9 jit_solution(10404148225332691174)
XLA Ops:
  0.7 80.2 %correlate.1 = (bf16[24,128,1024]{2,1,0:T(8,128)(2,1)}, bf16[3,8,256,128]{3,2,1,0:T(8,128)(2,1)}) custom-call(s32[1]{0:T(128)S(6)} %copy.7.starts_hbm, bf16[128,2304]{1,0:T(8,128)(2,1)} %traces_hbm.1, s32[1,128]{1,0:T(1,128)} %bitcast.4, s32[1,3]{1,0:T(1,128)} %offsets_hbm.1, bf16[2048,1024]{1,0:T(8,128)(2,1)} %constant.5.clone.basis_hbm, ...), custom_call_target="tpu_custom_call" | custom-call | tf_op jit(solution)/shard_map/correlate/pallas_call | solution.py:381
  80.8 7.0 %finish.1 = bf16[24,128,1024]{2,1,0:T(8,128)(2,1)} custom-call(bf16[24,128,1024]{2,1,0:T(8,128)(2,1)} %get-tuple-element.7.sums_hbm, bf16[24,256,128]{2,1,0:T(8,128)(2,1)} %bitcast.3, bf16[1024,1024]{1,0:T(8,128)(2,1)} %constant.4.clone.lag_hbm), custom_call_target="tpu_custom_call" | custom-call | tf_op jit(solution)/shard_map/finish/pallas_call | solution.py:448
